TPU v7x, 128 devices: a whole 4x4x4 slice. The times are simulated.
128 devices in a mesh: layer: 2 (over core), row: 4 (over z), col: 16 (over x, y).
Axes of the slice: x: 4, y: 4, z: 4, core: 2. Of those that a mesh axis runs over, the one named last changes fastest.
Arguments:
- iterate: bfloat16 [10752, 12288], P(('layer', 'row'), 'col'), parts along dimension 0, may hold values from -0.026062528 to 0.026062528
Outputs:
- update: bfloat16 [10752, 12288], P(('layer', 'row'), 'col'), parts along dimension 0
There are 2 independent parts, one for each index of `layer`. A program takes and returns all parts, laid end to end along the dimension named above; each array names one. Nothing has to cross between parts.
All inputs are finite; a program needn't handle non-finite values.
Results may differ from a plain program's by a relative error of at most 0.024.
Values may be sent and summed in bfloat16 or wider, within the bound.
A program may use at most 128 MiB of HBM per device.

v0:
```python
import math

import jax
import jax.numpy as jnp
from jax import lax
from jax.sharding import PartitionSpec as P

M = 5376
N = 12288


coef_linear = 3.4445
coef_cubic = -4.775
coef_quintic = 2.0315


def round_term(value):
    rounded = lax.optimization_barrier(value.astype(jnp.bfloat16))
    return rounded.astype(jnp.float32)


def on_device(iterate):
    panel = lax.all_gather(iterate, "row", axis=0, tiled=True)
    total_rows = panel.shape[0]
    slab = total_rows // lax.axis_size("col")
    contract = (((1,), (1,)), ((), ()))
    partial_value = round_term(
        lax.dot_general(iterate, panel, contract, preferred_element_type=jnp.float32)
    )
    gram_rows = lax.psum(partial_value.astype(jnp.bfloat16), "col")
    col_start = lax.axis_index("col") * slab
    gram_tile = lax.dynamic_slice_in_dim(gram_rows, col_start, slab, 1)
    column_block = lax.all_gather(gram_tile, "row", axis=0, tiled=True)
    gram_square = jnp.dot(gram_rows, column_block, preferred_element_type=jnp.float32)
    poly_tile = (coef_cubic * gram_tile.astype(jnp.float32) + coef_quintic * gram_square).astype(
        jnp.bfloat16
    )
    product = jnp.dot(
        lax.all_gather(poly_tile, "col", axis=1, tiled=True),
        panel,
        preferred_element_type=jnp.float32,
    )
    factor = 0.2 * math.sqrt(max(M, N))
    return (factor * (coef_linear * iterate.astype(jnp.float32) + product)).astype(jnp.bfloat16)


def solution(mesh):
    return jax.shard_map(
        on_device,
        mesh=mesh,
        in_specs=(P(("layer", "row"), "col"),),
        out_specs=P(("layer", "row"), "col"),
        check_vma=False,
    )
```

profile of v0, /device:TPU:0, one launch (start us, length us, event | category | flops | bytes accessed | tf_op | source)
XLA Modules:
  0.0 520.2 jit_solution(1838182831054957089)
XLA Ops:
  6.5 0.0 all-gather.5.cloned.1.call-start
  6.5 0.7 all-gather.5.cloned.1.call-update
  7.3 0.0 all-reduce.2.cloned.1.call-start
  7.3 86.5 %all-gather.5.cloned.1.call-done = bf16[5376,768]{1,0:T(8,128)(2,1)} async-done(((bf16[1344,768]{1,0:T(8,128)(2,1)}), bf16[5376,768]{1,0:T(8,128)(2,1)}) %all-gather.5.cloned.1.call-update) | async-done | bytes 8257552 | tf_op jit(solution)/shard_map/all_gather | solution.py:23
  93.8 19.2 %convolution_convert_fusion = bf16[1344,5376]{0,1:T(8,128)(2,1)} fusion(bf16[1344,768]{1,0:T(8,128)(2,1)} %param.1, bf16[5376,768]{1,0:T(8,128)(2,1)} %all-gather.5.cloned.1.call-done), kind=kOutput, calls=%fused_computation | convolution fusion | flops 11105353728 | bytes 24772608 | tf_op jit(solution)/shard_map/dot_general | solution.py:28
  113.0 0.0 all-reduce.2.cloned.1.call-update
  113.0 0.0 all-gather.9.cloned.1.call-start
  113.1 204.9 %all-reduce.2.cloned.1.call-done = bf16[1344,5376]{0,1:T(8,128)(2,1)} async-done(((bf16[1344,5376]{0,1:T(8,128)(2,1)}), bf16[1344,5376]{0,1:T(8,128)(2,1)}) %all-reduce.2.cloned.1.call-update) | async-done | bytes 14450704 | tf_op jit(solution)/shard_map/psum | solution.py:30
  318.0 2.2 dynamic-slice_bitcast_fusion
  320.2 0.0 all-gather.9.cloned.1.call-update
  320.2 0.2 all-gather.7.cloned.1.call-start
  320.4 44.8 %all-gather.9.cloned.1.call-done = bf16[4,1344,336]{1,2,0:T(8,128)(2,1)} async-done(((bf16[1,1344,336]{1,2,0:T(8,128)(2,1)}), bf16[4,1344,336]{1,2,0:T(8,128)(2,1)}) %all-gather.9.cloned.1.call-update) | async-done | bytes 3612688 | tf_op jit(solution)/shard_map/all_gather | solution.py:33
  365.2 5.4 %copy.8 = bf16[4,1344,336]{1,0,2:T(4,128)(2,1)} copy(bf16[4,1344,336]{1,2,0:T(8,128)(2,1)} %all-gather.9.cloned.1.call-done) | data formatting | bytes 7225344 | tf_op jit(solution)/shard_map/all_gather | solution.py:33
  370.6 7.4 %reshape.1 = bf16[5376,336]{0,1:T(8,128)(2,1)} reshape(bf16[4,1344,336]{1,0,2:T(4,128)(2,1)} %copy.8) | data formatting | bytes 7225344
  378.0 0.0 copy-start
  378.0 13.2 %fusion.1 = bf16[1344,336]{0,1:T(8,128)(2,1)} fusion(bf16[5376,336]{0,1:T(8,128)(2,1)} %reshape.1, bf16[1344,5376]{0,1:T(8,128)(2,1)} %all-reduce.2.cloned.1.call-done, s32[]{:T(128)S(6)} %select_n.3), kind=kOutput, calls=%fused_computation.4 | convolution fusion | flops 4857689088 | bytes 20600836 | tf_op jit(solution)/shard_map/dot_general | solution.py:34
  391.2 0.0 all-gather.7.cloned.1.call-update
  391.2 102.8 %all-gather.7.cloned.1.call-done = bf16[1344,5376]{0,1:T(8,128)(2,1)} async-done(((bf16[1344,336]{0,1:T(8,128)(2,1)}), bf16[1344,5376]{0,1:T(8,128)(2,1)}) %all-gather.7.cloned.1.call-update) | async-done | bytes 14450704 | tf_op jit(solution)/shard_map/all_gather | solution.py:39
  494.0 0.0 copy-done
  494.0 19.7 %multiply_convert_fusion = bf16[1344,768]{1,0:T(8,128)(2,1)} fusion(bf16[1344,768]{1,0:T(8,128)(2,1)S(1)} %copy-done, bf16[1344,5376]{0,1:T(8,128)(2,1)} %all-gather.7.cloned.1.call-done, bf16[5376,768]{1,0:T(8,128)(2,1)} %all-gather.5.cloned.1.call-done), kind=kOutput, calls=%fused_computation.1 | convolution fusion | flops 11103289344 | bytes 26836992 | tf_op jit(solution)/shard_map/dot_general | solution.py:38
Async XLA Ops:
  6.5 87.3 %all-gather.5.cloned.1.call-start = ((), (), s32[]{:S(2)}) async-start(), calls=%async_computation | async-start | bytes 10321920 | tf_op jit(solution)/shard_map/all_gather | solution.py:23
  7.3 310.7 %all-reduce.2.cloned.1.call-start = ((), (), s32[]{:S(2)}) async-start(), calls=%async_computation.1 | async-start | bytes 30277632 | tf_op jit(solution)/shard_map/psum | solution.py:30
  113.0 252.2 %all-gather.9.cloned.1.call-start = ((), (), s32[]{:S(2)}) async-start(), calls=%async_computation.3 | async-start | bytes 4730880 | tf_op jit(solution)/shard_map/all_gather | solution.py:33
  320.2 173.9 %all-gather.7.cloned.1.call-start = ((), (), s32[]{:S(2)}) async-start(), calls=%async_computation.2 | async-start | bytes 16084992 | tf_op jit(solution)/shard_map/all_gather | solution.py:39
  378.0 116.1 %copy-start = (bf16[1344,768]{1,0:T(8,128)(2,1)S(1)}, bf16[1344,768]{1,0:T(8,128)(2,1)}, u32[]{:S(2)}) copy-start(bf16[1344,768]{1,0:T(8,128)(2,1)} %param.1) | copy-start | bytes 6193156
Sparse Core Ops, SparseCore 0:
  9.0 84.7 all-gather.4
  113.1 204.7 all-reduce.1
  320.3 44.9 all-gather.8
  391.3 102.6 all-gather.6
where the time goes:
time: 521 us; the launch traced here: 520 us
  waiting for transfers between devices  440 us (84%)
  matrix products  52.1 us (10%)
  local copies, waits for them, and re-layouts  14.9 us (3%)
  between operations  13.1 us (3%)
    psum x1, waiting for transfers between devices, on_device(): gram_rows = lax.psum(partial_value.astype(jnp.bfloat16), 'col')  205 us
    all_gather x1, waiting for transfers between devices, on_device(): lax.all_gather(poly_tile, 'col', axis=1, tiled=True)  103 us
    all_gather x1, waiting for transfers between devices, on_device(): panel = lax.all_gather(iterate, 'row', axis=0, tiled=True)  86.5 us
    all_gather x1, waiting for transfers between devices, on_device(): column_block = lax.all_gather(gram_tile, 'row', axis=0, tiled=True)  44.8 us
    dot_general x1, matrix products, on_device(): jnp.dot(lax.all_gather(poly_tile, 'col', axis=1, tiled=True), panel, pref...  19.7 us
    dot_general x1, matrix products, on_device(): lax.dot_general(iterate, panel, contract, preferred_element_type=jnp.floa...  19.2 us
    dot_general x1, matrix products, on_device(): jnp.dot(gram_rows, column_block, preferred_element_type=jnp.float32)  13.2 us
  transfers between devices with their start and end apart: 4, of which 4 were waited for; matrix products, arithmetic and copies ran while one was open for 0% of the time, Pallas kernels for 0%

commit v1 on v0

v1 whole, which is shorter than its diff:
```python
import math

import jax
import jax.numpy as jnp
from jax import lax
from jax.sharding import PartitionSpec as P

M = 5376
N = 12288


coef_linear = 3.4445
coef_cubic = -4.775
coef_quintic = 2.0315


def on_device(iterate):
    panel = lax.all_gather(iterate, "row", axis=0, tiled=True)
    contract = (((1,), (1,)), ((), ()))
    partial_value = lax.dot_general(
        iterate, panel, contract, preferred_element_type=jnp.float32
    ).astype(jnp.bfloat16)
    gram_rows = lax.psum(partial_value, "col")
    once = jnp.dot(gram_rows, panel, preferred_element_type=jnp.float32)
    once_panel = lax.all_gather(once.astype(jnp.bfloat16), "row", axis=0, tiled=True)
    twice = jnp.dot(gram_rows, once_panel, preferred_element_type=jnp.float32)
    product = coef_cubic * once + coef_quintic * twice
    factor = 0.2 * math.sqrt(max(M, N))
    return (factor * (coef_linear * iterate.astype(jnp.float32) + product)).astype(jnp.bfloat16)


def solution(mesh):
    return jax.shard_map(
        on_device,
        mesh=mesh,
        in_specs=(P(("layer", "row"), "col"),),
        out_specs=P(("layer", "row"), "col"),
        check_vma=False,
    )
```

time: 521 us -> 436 us (0.84)
  waiting for transfers between devices: 440 us -> 368 us
  local copies, waits for them, and re-layouts: 14.9 us -> 0.01 us
    all_gather x2 -> x1, waiting for transfers between devices: 148 us -> 82.2 us  [on_device(): lax.all_gather(once.astype(jnp.bfloat16), 'row', axis=0, tiled=True)]
    unnamed x4 -> x2, local copies, waits for them, and re-layouts: 9.55 us -> 0.01 us
    psum x1, waiting for transfers between devices: 205 us -> 198 us  [on_device(): gram_rows = lax.psum(partial_value, 'col')]
    all_gather x1 -> x0, local copies, waits for them, and re-layouts: 5.36 us -> none  [on_device(): column_block = lax.all_gather(gram_tile, 'row', axis=0, tiled=True)]
  transfers between devices with their start and end apart: 4 -> 3, of which waited for: 4 -> 3; matrix products, arithmetic and copies ran while one was open for 0% -> 0% of each run, Pallas kernels for 0% -> 0%
where the time goes in v1:
time: 436 us
  waiting for transfers between devices  368 us (84%)
  matrix products  54.9 us (13%)
  between operations  13.1 us (3%)
    psum x1, waiting for transfers between devices, on_device(): gram_rows = lax.psum(partial_value, 'col')  198 us
    all_gather x1, waiting for transfers between devices, on_device(): panel = lax.all_gather(iterate, 'row', axis=0, tiled=True)  86.5 us
    all_gather x1, waiting for transfers between devices, on_device(): lax.all_gather(once.astype(jnp.bfloat16), 'row', axis=0, tiled=True)  82.2 us
    dot_general x1, matrix products, on_device(): twice = jnp.dot(gram_rows, once_panel, preferred_element_type=jnp.float32)  18.8 us
    dot_general x1, matrix products, on_device(): lax.dot_general(iterate, panel, contract, preferred_element_type=jnp.floa...  18.2 us
    dot_general x1, matrix products, on_device(): once = jnp.dot(gram_rows, panel, preferred_element_type=jnp.float32)  17.8 us
  transfers between devices with their start and end apart: 3, of which 3 were waited for; matrix products, arithmetic and copies ran while one was open for 0% of the time, Pallas kernels for 0%

profile of v1, /device:TPU:0, one launch (start us, length us, event | category | flops | bytes accessed | tf_op | source)
XLA Modules:
  0.0 435.6 jit_solution(16978007294724145178)
XLA Ops:
  6.5 0.0 all-gather.3.cloned.1.call-start
  6.5 0.7 all-gather.3.cloned.1.call-update
  7.3 0.0 all-reduce.2.cloned.1.call-start
  7.3 86.5 %all-gather.3.cloned.1.call-done = bf16[5376,768]{1,0:T(8,128)(2,1)} async-done(((bf16[1344,768]{1,0:T(8,128)(2,1)}), bf16[5376,768]{1,0:T(8,128)(2,1)}) %all-gather.3.cloned.1.call-update) | async-done | bytes 8257552 | tf_op jit(solution)/shard_map/all_gather | solution.py:18
  93.8 18.2 %convolution_convert_fusion = bf16[1344,5376]{1,0:T(8,128)(2,1)} fusion(bf16[1344,768]{1,0:T(8,128)(2,1)} %param.1, bf16[5376,768]{1,0:T(8,128)(2,1)} %all-gather.3.cloned.1.call-done), kind=kOutput, calls=%fused_computation | convolution fusion | flops 11105353728 | bytes 24772608 | tf_op jit(solution)/shard_map/dot_general | solution.py:20
  112.0 0.0 all-reduce.2.cloned.1.call-update
  112.0 0.0 copy-start
  112.0 0.0 all-gather.5.cloned.1.call-start
  112.1 198.1 %all-reduce.2.cloned.1.call-done = bf16[1344,5376]{1,0:T(8,128)(2,1)} async-done(((bf16[1344,5376]{1,0:T(8,128)(2,1)}), bf16[1344,5376]{1,0:T(8,128)(2,1)}) %all-reduce.2.cloned.1.call-update) | async-done | bytes 14450704 | tf_op jit(solution)/shard_map/psum | solution.py:23
  310.2 17.8 %fusion = (bf16[1344,768]{1,0:T(8,128)(2,1)}, f32[1344,768]{1,0:T(8,128)}) fusion(bf16[1344,5376]{1,0:T(8,128)(2,1)} %all-reduce.2.cloned.1.call-done, bf16[5376,768]{1,0:T(8,128)(2,1)} %all-gather.3.cloned.1.call-done), kind=kOutput, calls=%fused_computation.3 | convolution fusion | flops 11099160576 | bytes 28901376 | tf_op jit(solution)/shard_map/dot_general | solution.py:24
  328.0 0.0 all-gather.5.cloned.1.call-update
  328.0 82.2 %all-gather.5.cloned.1.call-done = bf16[5376,768]{1,0:T(8,128)(2,1)} async-done(((bf16[1344,768]{1,0:T(8,128)(2,1)}), bf16[5376,768]{1,0:T(8,128)(2,1)}) %all-gather.5.cloned.1.call-update) | async-done | bytes 8257552 | tf_op jit(solution)/shard_map/all_gather | solution.py:25
  410.3 0.0 copy-done
  410.3 18.8 %multiply_convert_fusion = bf16[1344,768]{1,0:T(8,128)(2,1)} fusion(f32[1344,768]{1,0:T(8,128)} %get-tuple-element.6, bf16[1344,768]{1,0:T(8,128)(2,1)S(1)} %copy-done, bf16[1344,5376]{1,0:T(8,128)(2,1)} %all-reduce.2.cloned.1.call-done, bf16[5376,768]{1,0:T(8,128)(2,1)} %all-gather.5.cloned.1.call-done), kind=kOutput, calls=%fused_computation.2 | convolution fusion | flops 11106385920 | bytes 30965760 | tf_op jit(solution)/shard_map/dot_general | solution.py:26
Async XLA Ops:
  6.5 87.3 %all-gather.3.cloned.1.call-start = ((), (), s32[]{:S(2)}) async-start(), calls=%async_computation | async-start | bytes 10321920 | tf_op jit(solution)/shard_map/all_gather | solution.py:18
  7.3 302.9 %all-reduce.2.cloned.1.call-start = ((), (), s32[]{:S(2)}) async-start(), calls=%async_computation.1 | async-start | bytes 28901376 | tf_op jit(solution)/shard_map/psum | solution.py:23
  112.0 298.3 %copy-start = (bf16[1344,768]{1,0:T(8,128)(2,1)S(1)}, bf16[1344,768]{1,0:T(8,128)(2,1)}, u32[]{:S(2)}) copy-start(bf16[1344,768]{1,0:T(8,128)(2,1)} %param.1) | copy-start | bytes 6193156
  112.0 298.2 %all-gather.5.cloned.1.call-start = ((), (), s32[]{:S(2)}) async-start(), calls=%async_computation.2 | async-start | bytes 10321920 | tf_op jit(solution)/shard_map/all_gather | solution.py:25
Sparse Core Ops, SparseCore 0:
  9.0 84.7 all-gather.2
  112.1 198.0 all-reduce.1
  328.1 82.0 all-gather.4

commit v2 on v1

v2 whole, which is shorter than its diff:
```python
import functools
import math

import jax
import jax.numpy as jnp
from jax import lax
from jax.experimental import pallas as pl
from jax.experimental.pallas import tpu as pltpu
from jax.sharding import PartitionSpec as P

M = 5376
N = 12288

coef_linear = 3.4445
coef_cubic = -4.775
coef_quintic = 2.0315
factor = 0.2 * math.sqrt(max(M, N))

BLOCK = 1344
CHUNK = 336
DEPTH = 768
WIDE = 1408
PIECE = 384
FULL = 4 * PIECE

PART_A = (0, 176)
PART_B = (176, 160)
HALF_AA = (0, 96)
HALF_AB = (96, 80)
HALF_BA = (176, 80)
HALF_BB = (256, 80)

TRANSPOSED = (((1,), (1,)), ((), ()))
COPIES = 240


def rows_of(part):
    return pl.ds(part[0], part[1])


def kernel(
    x_hbm, o_ref, xs, send, summed, got_far, got_near, got_piece, gram, ys, acc, y_acc,
    local_sem, send_sem, recv_sem,
):
    layer = lax.axis_index("layer")
    row = lax.axis_index("row")
    col = lax.axis_index("col")
    px = lax.div(col, 4)
    py = lax.rem(col, 4)
    pa = px * (1 - layer) + py * layer
    pb = py * (1 - layer) + px * layer

    def ring(position, step):
        return lax.rem(position + (step + 4), 4)

    def device(da=0, db=0, dz=0):
        na, nb = ring(pa, da), ring(pb, db)
        nx = na * (1 - layer) + nb * layer
        ny = nb * (1 - layer) + na * layer
        return (layer, ring(row, dz), nx * 4 + ny)

    used = [0]

    def start(src, dst, target):
        index = used[0]
        used[0] += 1
        copy = pltpu.make_async_remote_copy(
            src_ref=src,
            dst_ref=dst,
            send_sem=send_sem.at[index],
            recv_sem=recv_sem.at[index],
            device_id=target,
            device_id_type=pl.DeviceIdType.MESH,
        )
        copy.start()
        unsent.append(copy)
        return copy

    unsent = []

    def sent(copies):
        for copy in copies:
            copy.wait_send()
            unsent[:] = [other for other in unsent if other is not copy]

    def received(copies):
        for copy in copies:
            copy.wait_recv()

    partners = [device(dz=1), device(dz=-1)]
    for step in (1, 2, 3):
        partners += [device(da=step), device(db=step)]
    barrier = pltpu.get_barrier_semaphore()
    for partner in partners:
        pl.semaphore_signal(
            barrier, inc=1, device_id=partner, device_id_type=pl.DeviceIdType.MESH
        )
    own = pltpu.make_async_copy(x_hbm, xs.at[0], local_sem)
    own.start()
    pl.semaphore_wait(barrier, len(partners))

    low, high = pl.ds(0, BLOCK // 2), pl.ds(BLOCK // 2, BLOCK // 2)
    up_low = start(x_hbm.at[low], xs.at[3, low], device(dz=1))
    down_high = start(x_hbm.at[high], xs.at[1, high], device(dz=-1))
    up_high = start(x_hbm.at[high], xs.at[3, high], device(dz=1))
    down_low = start(x_hbm.at[low], xs.at[1, low], device(dz=-1))

    for k in range(2):
        summed[k, :, pl.ds(1280, FULL - 1280)] = jnp.zeros((CHUNK, FULL - 1280), jnp.bfloat16)
    own.wait()

    def base_a(slot):
        return pl.multiple_of(ring(pa, slot) * CHUNK, 16)

    def base_b(slot):
        return pl.multiple_of(ring(pb, slot) * CHUNK, 16)

    def gram_terms(slot, j):
        mine = jnp.concatenate(
            [
                xs[0, pl.ds(base_a(slot), PART_A[1]), :],
                xs[0, pl.ds(pl.multiple_of(base_b(slot) + PART_B[0], 16), PART_B[1]), :],
            ],
            axis=0,
        )
        return lax.dot_general(mine, xs[j], TRANSPOSED, preferred_element_type=jnp.float32)

    buffer_set = {0: 0, 1: 1, 3: 0, 2: 1}
    landing_set = {0: 0, 1: 1, 3: 2, 2: 0}
    from_buffer = {}
    step1, step2, step3, step4, step5, step6 = {}, {}, {}, {}, {}, {}
    body = pl.ds(0, BLOCK)
    wide = pl.ds(0, WIDE)

    def reuse(name, k):
        sent(from_buffer.pop((name, k), []))

    def phase1(j):
        k, q = buffer_set[j], landing_set[j]
        reuse("far", k)
        send[k, 0, :, body] = gram_terms(2, j).astype(jnp.bfloat16)
        step1[j] = []
        for half, target in (
            (HALF_AA, device(da=1)),
            (HALF_BA, device(db=1)),
            (HALF_AB, device(da=-1)),
            (HALF_BB, device(db=-1)),
        ):
            rows = rows_of(half)
            step1[j].append(start(send.at[k, 0, rows], got_far.at[q, rows], target))
        from_buffer["far", k] = list(step1[j])

    def phase2(j):
        k, q = buffer_set[j], landing_set[j]
        received(step1[j])
        step2[j] = []
        for side, slot, added in ((1, 1, (HALF_AA, HALF_BA)), (2, 3, (HALF_AB, HALF_BB))):
            reuse(side, k)
            terms = gram_terms(slot, j)
            for half in (HALF_AA, HALF_AB, HALF_BA, HALF_BB):
                rows = rows_of(half)
                value = terms[half[0] : half[0] + half[1], :]
                if half in added:
                    value = value + got_far[q, rows, body].astype(jnp.float32)
                send[k, side, rows, body] = value.astype(jnp.bfloat16)
            way = 1 if slot == 1 else -1
            copies = []
            for part, target in ((PART_A, device(da=way)), (PART_B, device(db=way))):
                rows = rows_of(part)
                copies.append(
                    start(send.at[k, side, rows], got_near.at[q, side - 1, rows], target)
                )
            from_buffer[side, k] = copies
            step2[j] += copies

    def piece(position):
        return pl.ds(pl.multiple_of(position * PIECE, 128), PIECE)

    def phase3(j):
        k, q = buffer_set[j], landing_set[j]
        terms = gram_terms(0, j)
        received(step2[j])
        reuse("sum", k)
        summed[k, :, body] = (
            terms
            + got_near[q, 0, :, body].astype(jnp.float32)
            + got_near[q, 1, :, body].astype(jnp.float32)
        ).astype(jnp.bfloat16)
        step3[j] = []
        for step in (2, 1, 3):
            for part, place, target in (
                (PART_A, ring(pb, step), device(db=step)),
                (PART_B, ring(pa, step), device(da=step)),
            ):
                rows = rows_of(part)
                step3[j].append(
                    start(
                        summed.at[k, rows, piece(place)],
                        got_piece.at[q, step - 1, rows],
                        target,
                    )
                )
        from_buffer["sum", k] = list(step3[j])

    def phase4(j):
        k, q = buffer_set[j], landing_set[j]
        received(step3[j])
        for part, place in ((PART_A, pb), (PART_B, pa)):
            rows = rows_of(part)
            value = summed[k, rows, piece(place)].astype(jnp.float32)
            for step in range(3):
                value = value + got_piece[q, step, rows, :].astype(jnp.float32)
            gram[0, j, rows, piece(place)] = value.astype(jnp.bfloat16)
        step4[j] = []
        for step in (2, 1, 3):
            for part, place, target in (
                (PART_A, pb, device(db=step)),
                (PART_B, pa, device(da=step)),
            ):
                where = gram.at[0, j, rows_of(part), piece(place)]
                step4[j].append(start(where, where, target))

    def phase5(j, half):
        if half == 0:
            received(step4[j])
            step5[j] = []
        copies = []
        for rows_half, target_up, target_down in (
            ((HALF_AA, HALF_AB)[half], device(da=1), device(da=-1)),
            ((HALF_BA, HALF_BB)[half], device(db=1), device(db=-1)),
        ):
            rows = rows_of(rows_half)
            src = gram.at[0, j, rows, wide]
            copies.append(start(src, gram.at[3, j, rows, wide], target_up))
            copies.append(start(src, gram.at[1, j, rows, wide], target_down))
        step5[j].append(copies)

    def phase6(j, half):
        received(step5[j][half])
        if half == 0:
            step6[j] = []
        for rows_half, target in (
            ((HALF_AA, HALF_AB)[half], device(da=(1, -1)[half])),
            ((HALF_BA, HALF_BB)[half], device(db=(1, -1)[half])),
        ):
            rows = rows_of(rows_half)
            step6[j].append(
                start(
                    gram.at[(3, 1)[half], j, rows, wide], gram.at[2, j, rows, wide], target
                )
            )

    def place_of(slot, part):
        base = base_a(slot) if part[0] < PART_B[0] else base_b(slot)
        return pl.ds(pl.multiple_of(base + part[0], 16), part[1])

    direct, forward = {}, {}

    def once(name, pieces):
        total = sum(part[1] for _, part in pieces)

        def add(j, carry):
            left = [gram[slot, j, rows_of(part), body] for slot, part in pieces]
            left = left[0] if len(left) == 1 else jnp.concatenate(left, axis=0)
            term = jnp.dot(left, xs[j], preferred_element_type=jnp.float32)

            @pl.when(j == 0)
            def _():
                y_acc[pl.ds(0, total), :] = term

            @pl.when(j != 0)
            def _():
                y_acc[pl.ds(0, total), :] += term

            return carry

        lax.fori_loop(0, 4, add, 0)
        offset = 0
        for slot, part in pieces:
            value = y_acc[pl.ds(offset, part[1]), :]
            offset += part[1]
            place = place_of(slot, part)
            acc[slot, rows_of(part), :] = (
                coef_linear * xs[0, place, :].astype(jnp.float32) + coef_cubic * value
            )
            ys[0, place, :] = value.astype(jnp.bfloat16)
        direct[name] = []
        for slot, part in pieces:
            place = place_of(slot, part)
            src = ys.at[0, place]
            direct[name].append(
                (
                    slot,
                    part,
                    start(src, ys.at[3, place], device(dz=1)),
                    start(src, ys.at[1, place], device(dz=-1)),
                )
            )

    def pass_on(name):
        forward[name] = []
        for slot, part, up, down in direct[name]:
            place = place_of(slot, part)
            received([up, down])
            if part[0] < PART_B[0]:
                copy = start(ys.at[3, place], ys.at[2, place], device(dz=1))
            else:
                copy = start(ys.at[1, place], ys.at[2, place], device(dz=-1))
            forward[name].append(copy)

    def twice(j, last=False):
        def add(slot, carry):
            term = jnp.dot(gram[slot, j, :, body], ys[j], preferred_element_type=jnp.float32)
            value = acc[slot] + coef_quintic * term
            if last:
                value = (factor * value).astype(jnp.bfloat16)
                for part in (PART_A, PART_B):
                    o_ref[place_of(slot, part), :] = value[part[0] : part[0] + part[1], :]
            else:
                acc[slot] = value
            return carry

        lax.fori_loop(0, 4, add, 0)

    phase1(0)
    phase2(0)
    phase3(0)
    phase4(0)
    received([up_low])
    far_low = start(xs.at[3, low], xs.at[2, low], device(dz=1))
    received([down_high])
    far_high = start(xs.at[1, high], xs.at[2, high], device(dz=-1))
    phase5(0, 0)
    phase5(0, 1)
    phase6(0, 0)
    phase6(0, 1)
    received([down_low])
    phase1(1)
    received([up_high])
    phase1(3)
    phase2(1)
    phase2(3)
    received([far_low, far_high])
    phase1(2)
    phase3(1)
    phase3(3)
    phase2(2)
    phase4(1)
    phase4(3)
    phase3(2)
    phase5(1, 0)
    phase5(3, 0)
    phase4(2)
    received(step6[0])
    phase5(2, 0)
    phase5(1, 1)
    phase5(3, 1)
    phase5(2, 1)
    once("own", ((0, PART_A), (0, PART_B)))
    phase6(1, 0)
    phase6(3, 0)
    phase6(2, 0)
    once("first", ((1, HALF_AA), (3, HALF_AA), (1, HALF_BA), (3, HALF_BA)))
    pass_on("own")
    phase6(1, 1)
    phase6(3, 1)
    phase6(2, 1)
    once("second", ((1, HALF_AB), (3, HALF_AB), (1, HALF_BB), (3, HALF_BB)))
    pass_on("first")
    for j in (1, 3, 2):
        received(step6[j])
    once("last", ((2, PART_A), (2, PART_B)))
    pass_on("second")
    twice(0)
    pass_on("last")
    twice(1)
    twice(3)
    for name in ("own", "first", "second", "last"):
        received(forward[name])
    twice(2, last=True)
    sent(list(unsent))


def on_device(iterate):
    any_space = pl.BlockSpec(memory_space=pl.ANY)
    vmem = pl.BlockSpec(memory_space=pltpu.VMEM)
    bf16 = jnp.bfloat16
    return pl.pallas_call(
        kernel,
        out_shape=jax.ShapeDtypeStruct((BLOCK, DEPTH), bf16),
        in_specs=[any_space],
        out_specs=vmem,
        scratch_shapes=[
            pltpu.VMEM((4, BLOCK, DEPTH), bf16),
            pltpu.VMEM((2, 3, CHUNK, WIDE), bf16),
            pltpu.VMEM((2, CHUNK, FULL), bf16),
            pltpu.VMEM((3, CHUNK, WIDE), bf16),
            pltpu.VMEM((3, 2, CHUNK, WIDE), bf16),
            pltpu.VMEM((3, 3, CHUNK, PIECE), bf16),
            pltpu.VMEM((4, 4, CHUNK, FULL), bf16),
            pltpu.VMEM((4, BLOCK, DEPTH), bf16),
            pltpu.VMEM((4, CHUNK, DEPTH), jnp.float32),
            pltpu.VMEM((352, DEPTH), jnp.float32),
            pltpu.SemaphoreType.DMA,
            pltpu.SemaphoreType.DMA((COPIES,)),
            pltpu.SemaphoreType.DMA((COPIES,)),
        ],
        compiler_params=pltpu.CompilerParams(
            collective_id=0, has_side_effects=True, vmem_limit_bytes=63 * 2**20
        ),
        name="newton_schulz",
    )(iterate)


def solution(mesh):
    return jax.shard_map(
        on_device,
        mesh=mesh,
        in_specs=(P(("layer", "row"), "col"),),
        out_specs=P(("layer", "row"), "col"),
        check_vma=False,
    )
```

time: 436 us -> 242 us (0.56)
  waiting for transfers between devices: 368 us -> 0 us
  Pallas kernels: 0 us -> 238 us
  matrix products: 54.9 us -> 0 us
  between operations: 13.1 us -> 0.01 us
    pallas_call x0 -> x1, Pallas kernels: none -> 238 us  [on_device(): pl.pallas_call(kernel, out_shape=jax.ShapeDtypeStruct((BLOCK, DEPTH), bf1...]
    psum x1 -> x0, waiting for transfers between devices: 198 us -> none  [on_device(): gram_rows = lax.psum(partial_value, 'col')]
    all_gather x2 -> x0, waiting for transfers between devices: 169 us -> none  [the longest x1 86.5 us: on_device(): panel = lax.all_gather(iterate, 'row', axis=0, tiled=True)]
    dot_general x3 -> x0, matrix products: 54.9 us -> none  [the longest x1 18.8 us: on_device(): twice = jnp.dot(gram_rows, once_panel, preferred_element_type=jnp.float32)]
  transfers between devices with their start and end apart: 3 -> 0, of which waited for: 3 -> 0; matrix products, arithmetic and copies ran while one was open for 0% -> 0% of each run, Pallas kernels for 0% -> 0%
where the time goes in v2:
time: 242 us; the launch traced here: 241 us
  Pallas kernels  238 us (98%)
  local copies, waits for them, and re-layouts  3.02 us (1%)
    pallas_call x1, Pallas kernels, on_device(): pl.pallas_call(kernel, out_shape=jax.ShapeDtypeStruct((BLOCK, DEPTH), bf1...  238 us

profile of v2, /device:TPU:0, one launch (start us, length us, event | category | flops | bytes accessed | tf_op | source)
XLA Modules:
  0.0 240.9 jit_solution(18157963945326421789)
XLA Ops:
  0.0 237.9 %newton_schulz.1 = bf16[1344,768]{1,0:T(8,128)(2,1)} custom-call(bf16[1344,768]{1,0:T(8,128)(2,1)} %x_hbm.1), custom_call_target="tpu_custom_call" | custom-call | tf_op jit(solution)/shard_map/newton_schulz/pallas_call | solution.py:388
  237.9 3.0 %copy.3 = bf16[1344,768]{1,0:T(8,128)(2,1)} copy(bf16[1344,768]{1,0:T(8,128)(2,1)} %newton_schulz.1) | data formatting | bytes 4128768

commit v3 on v2

v3 whole, which is shorter than its diff:
```python
import functools
import math

import jax
import jax.numpy as jnp
from jax import lax
from jax.experimental import pallas as pl
from jax.experimental.pallas import tpu as pltpu
from jax.sharding import PartitionSpec as P

M = 5376
N = 12288

coef_linear = 3.4445
coef_cubic = -4.775
coef_quintic = 2.0315
factor = 0.2 * math.sqrt(max(M, N))

BLOCK = 1344
CHUNK = 336
SPLIT = 640
DEPTH = 768
WIDE = 1408
PIECE = 384
FULL = 4 * PIECE

PART_A = (0, 176)
PART_B = (176, 160)
HALF_AA = (0, 96)
HALF_AB = (96, 80)
HALF_BA = (176, 80)
HALF_BB = (256, 80)

TRANSPOSED = (((1,), (1,)), ((), ()))
LEFT_TRANSPOSED = (((0,), (0,)), ((), ()))
COPIES = 200


def rows_of(part):
    return pl.ds(part[0], part[1])


def kernel(
    x_hbm, o_ref, xs, send, summed, got_far, got_near, got_piece, gram, ys, acc, y_acc,
    local_sem, send_sem, recv_sem,
):
    layer = lax.axis_index("layer")
    row = lax.axis_index("row")
    col = lax.axis_index("col")
    px = lax.div(col, 4)
    py = lax.rem(col, 4)
    pa = px * (1 - layer) + py * layer
    pb = py * (1 - layer) + px * layer

    def ring(position, step):
        return lax.rem(position + (step + 4), 4)

    def device(da=0, db=0, dz=0):
        na, nb = ring(pa, da), ring(pb, db)
        nx = na * (1 - layer) + nb * layer
        ny = nb * (1 - layer) + na * layer
        return (layer, ring(row, dz), nx * 4 + ny)

    used = [0]

    def start(src, dst, target):
        index = used[0]
        used[0] += 1
        copy = pltpu.make_async_remote_copy(
            src_ref=src,
            dst_ref=dst,
            send_sem=send_sem.at[index],
            recv_sem=recv_sem.at[index],
            device_id=target,
            device_id_type=pl.DeviceIdType.MESH,
        )
        copy.start()
        unsent.append(copy)
        return copy

    unsent = []

    def sent(copies):
        for copy in copies:
            copy.wait_send()
            unsent[:] = [other for other in unsent if other is not copy]

    def received(copies):
        for copy in copies:
            copy.wait_recv()

    partners = [device(dz=1), device(dz=-1)]
    for step in (1, 2, 3):
        partners += [device(da=step), device(db=step)]
    barrier = pltpu.get_barrier_semaphore()
    for partner in partners:
        pl.semaphore_signal(
            barrier, inc=1, device_id=partner, device_id_type=pl.DeviceIdType.MESH
        )
    own = pltpu.make_async_copy(x_hbm, xs.at[0], local_sem)
    own.start()
    pl.semaphore_wait(barrier, len(partners))

    low, high = pl.ds(0, SPLIT), pl.ds(SPLIT, BLOCK - SPLIT)
    down_low = start(x_hbm.at[low], xs.at[1, low], device(dz=-1))
    up_high = start(x_hbm.at[high], xs.at[3, high], device(dz=1))
    down_high = start(x_hbm.at[high], xs.at[1, high], device(dz=-1))

    for k in range(2):
        summed[k, :, pl.ds(1280, FULL - 1280)] = jnp.zeros((CHUNK, FULL - 1280), jnp.bfloat16)
    own.wait()

    def place_of(slot, part):
        position = pa if part[0] < PART_B[0] else pb
        return pl.ds(pl.multiple_of(ring(position, slot) * CHUNK + part[0], 16), part[1])

    def slot_rows(ref, j, slot):
        return jnp.concatenate(
            [ref[j, place_of(slot, PART_A), :], ref[j, place_of(slot, PART_B), :]], axis=0
        )

    def gram_terms(slot, j, columns):
        return lax.dot_general(
            slot_rows(xs, 0, slot), xs[j, columns, :], TRANSPOSED,
            preferred_element_type=jnp.float32,
        )

    buffer_set = {0: 0, 1: 1, 2: 0}
    from_buffer = {}
    step1, step2, step3, step4, step5, step6 = {}, {}, {}, {}, {}, {}
    body = pl.ds(0, BLOCK)
    wide = pl.ds(0, WIDE)
    halves = (low, high)
    wide_halves = (low, pl.ds(SPLIT, WIDE - SPLIT))

    def reuse(name, j):
        key = name, buffer_set[j]
        owner, copies = from_buffer.get(key, (j, []))
        if owner != j:
            sent(copies)
            copies = []
        from_buffer[key] = (j, copies)
        return copies

    def phase1(j, h):
        k = buffer_set[j]
        copies = reuse("far", j)
        send[k, 0, :, halves[h]] = gram_terms(2, j, halves[h]).astype(jnp.bfloat16)
        step1[j, h] = []
        for half, target in (
            (HALF_AA, device(da=1)),
            (HALF_BA, device(db=1)),
            (HALF_AB, device(da=-1)),
            (HALF_BB, device(db=-1)),
        ):
            rows = rows_of(half)
            step1[j, h].append(
                start(
                    send.at[k, 0, rows, wide_halves[h]],
                    got_far.at[k, rows, wide_halves[h]],
                    target,
                )
            )
        copies += step1[j, h]

    def phase2(j, h):
        k = buffer_set[j]
        received(step1[j, h])
        step2[j, h] = []
        for side, slot, added in ((1, 1, (HALF_AA, HALF_BA)), (2, 3, (HALF_AB, HALF_BB))):
            copies = reuse(side, j)
            terms = gram_terms(slot, j, halves[h])
            for half in (HALF_AA, HALF_AB, HALF_BA, HALF_BB):
                rows = rows_of(half)
                value = terms[half[0] : half[0] + half[1], :]
                if half in added:
                    value = value + got_far[k, rows, halves[h]].astype(jnp.float32)
                send[k, side, rows, halves[h]] = value.astype(jnp.bfloat16)
            way = 1 if slot == 1 else -1
            for part, target in ((PART_A, device(da=way)), (PART_B, device(db=way))):
                rows = rows_of(part)
                copy = start(
                    send.at[k, side, rows, wide_halves[h]],
                    got_near.at[k, side - 1, rows, wide_halves[h]],
                    target,
                )
                copies.append(copy)
                step2[j, h].append(copy)

    def piece(position):
        return pl.ds(pl.multiple_of(position * PIECE, 128), PIECE)

    def phase3(j):
        k = buffer_set[j]
        copies = reuse("sum", j)
        for h in (0, 1):
            terms = gram_terms(0, j, halves[h])
            received(step2[j, h])
            summed[k, :, halves[h]] = (
                terms
                + got_near[k, 0, :, halves[h]].astype(jnp.float32)
                + got_near[k, 1, :, halves[h]].astype(jnp.float32)
            ).astype(jnp.bfloat16)
        step3[j] = []
        for step in (2, 1, 3):
            for part, place, target in (
                (PART_A, ring(pb, step), device(db=step)),
                (PART_B, ring(pa, step), device(da=step)),
            ):
                rows = rows_of(part)
                step3[j].append(
                    start(
                        summed.at[k, rows, piece(place)],
                        got_piece.at[k, step - 1, rows],
                        target,
                    )
                )
        copies += step3[j]

    def spread(j):
        step4[j] = []
        for step in (2, 1, 3):
            for part, place, target in (
                (PART_A, pb, device(db=step)),
                (PART_B, pa, device(da=step)),
            ):
                where = gram.at[0, j, rows_of(part), piece(place)]
                step4[j].append(start(where, where, target))

    def phase4(j):
        k = buffer_set[j]
        received(step3[j])
        for part, place in ((PART_A, pb), (PART_B, pa)):
            rows = rows_of(part)
            value = summed[k, rows, piece(place)].astype(jnp.float32)
            for step in range(3):
                value = value + got_piece[k, step, rows, :].astype(jnp.float32)
            gram[0, j, rows, piece(place)] = value.astype(jnp.bfloat16)
        if j == 1:
            for part, place in ((PART_A, pb), (PART_B, pa)):
                rows = rows_of(part)
                mirrored.append(
                    start(
                        gram.at[0, 1, rows, piece(place)],
                        gram.at[0, 3, rows, piece(place)],
                        device(dz=1),
                    )
                )
        spread(j)

    mirrored = []

    def phase5(j, half):
        if half == 0:
            received(step4[j])
            step5[j] = []
        copies = []
        for rows_half, target_up, target_down in (
            ((HALF_AA, HALF_AB)[half], device(da=1), device(da=-1)),
            ((HALF_BA, HALF_BB)[half], device(db=1), device(db=-1)),
        ):
            rows = rows_of(rows_half)
            src = gram.at[0, j, rows, wide]
            copies.append(start(src, gram.at[3, j, rows, wide], target_up))
            copies.append(start(src, gram.at[1, j, rows, wide], target_down))
        step5[j].append(copies)

    def phase6(j, half):
        received(step5[j][half])
        if half == 0:
            step6[j] = []
        for rows_half, target in (
            ((HALF_AA, HALF_AB)[half], device(da=(1, -1)[half])),
            ((HALF_BA, HALF_BB)[half], device(db=(1, -1)[half])),
        ):
            rows = rows_of(rows_half)
            step6[j].append(
                start(
                    gram.at[(3, 1)[half], j, rows, wide], gram.at[2, j, rows, wide], target
                )
            )

    direct, forward = {}, {}

    def mirrored_terms(slot, ref):
        return lax.dot_general(
            gram[slot, 3, :, body], slot_rows(ref, 3, slot), LEFT_TRANSPOSED,
            preferred_element_type=jnp.float32,
        )

    def once_mirrored():
        acc[...] = mirrored_terms(0, xs)

        def add(slot, carry):
            acc[...] += mirrored_terms(slot, xs)
            return carry

        lax.fori_loop(1, 4, add, 0)

    def once(name, pieces):
        total = sum(part[1] for _, part in pieces)

        def terms(j):
            left = [gram[slot, j, rows_of(part), body] for slot, part in pieces]
            left = left[0] if len(left) == 1 else jnp.concatenate(left, axis=0)
            return jnp.dot(left, xs[j], preferred_element_type=jnp.float32)

        y_acc[pl.ds(0, total), :] = terms(0)

        def add(j, carry):
            y_acc[pl.ds(0, total), :] += terms(j)
            return carry

        lax.fori_loop(1, 3, add, 0)
        offset = 0
        for slot, part in pieces:
            place = place_of(slot, part)
            value = y_acc[pl.ds(offset, part[1]), :] + acc[place, :]
            offset += part[1]
            acc[place, :] = coef_linear * xs[0, place, :].astype(jnp.float32) + coef_cubic * value
            ys[0, place, :] = value.astype(jnp.bfloat16)
        direct[name] = []
        for slot, part in pieces:
            place = place_of(slot, part)
            src = ys.at[0, place]
            direct[name].append(
                (
                    slot,
                    part,
                    start(src, ys.at[3, place], device(dz=1)),
                    start(src, ys.at[1, place], device(dz=-1)),
                )
            )

    def pass_on(name):
        forward[name] = []
        for slot, part, up, down in direct[name]:
            place = place_of(slot, part)
            received([up, down])
            if part[0] < PART_B[0]:
                copy = start(ys.at[3, place], ys.at[2, place], device(dz=1))
            else:
                copy = start(ys.at[1, place], ys.at[2, place], device(dz=-1))
            forward[name].append(copy)

    def twice(j, last=False):
        def add(slot, carry):
            term = coef_quintic * jnp.dot(
                gram[slot, j, :, body], ys[j], preferred_element_type=jnp.float32
            )
            for part in (PART_A, PART_B):
                place = place_of(slot, part)
                value = acc[place, :] + term[part[0] : part[0] + part[1], :]
                if last:
                    o_ref[place, :] = (factor * value).astype(jnp.bfloat16)
                else:
                    acc[place, :] = value
            return carry

        lax.fori_loop(0, 4, add, 0)

    def twice_mirrored():
        def add(slot, carry):
            acc[...] += coef_quintic * mirrored_terms(slot, ys)
            return carry

        lax.fori_loop(0, 4, add, 0)

    phase1(0, 0)
    phase1(0, 1)
    phase2(0, 0)
    phase2(0, 1)
    phase3(0)
    received([down_low])
    far_low = start(xs.at[1, low], xs.at[2, low], device(dz=-1))
    phase1(1, 0)
    received([up_high])
    far_high = start(xs.at[3, high], xs.at[2, high], device(dz=1))
    up_low = start(x_hbm.at[low], xs.at[3, low], device(dz=1))
    phase4(0)
    phase2(1, 0)
    phase5(0, 0)
    phase5(0, 1)
    received([down_high])
    phase1(1, 1)
    phase6(0, 0)
    phase6(0, 1)
    received([far_high])
    phase1(2, 1)
    phase2(1, 1)
    phase3(1)
    phase2(2, 1)
    phase4(1)
    received([far_low])
    phase1(2, 0)
    received(mirrored)
    spread(3)
    phase2(2, 0)
    phase5(3, 0)
    phase5(3, 1)
    phase3(2)
    phase6(3, 0)
    phase6(3, 1)
    phase4(2)
    phase5(1, 0)
    phase5(1, 1)
    received([up_low])
    received(step6[3])
    once_mirrored()
    phase5(2, 0)
    phase5(2, 1)
    received(step6[0])
    once("own", ((0, PART_A), (0, PART_B)))
    phase6(1, 0)
    phase6(2, 0)
    once("first", ((1, HALF_AA), (3, HALF_AA), (1, HALF_BA), (3, HALF_BA)))
    pass_on("own")
    phase6(1, 1)
    phase6(2, 1)
    once("second", ((1, HALF_AB), (3, HALF_AB), (1, HALF_BB), (3, HALF_BB)))
    pass_on("first")
    received(step6[1])
    received(step6[2])
    once("last", ((2, PART_A), (2, PART_B)))
    pass_on("second")
    twice(0)
    pass_on("last")
    twice_mirrored()
    twice(1)
    for name in ("own", "first", "second", "last"):
        received(forward[name])
    twice(2, last=True)
    sent(list(unsent))


def on_device(iterate):
    any_space = pl.BlockSpec(memory_space=pl.ANY)
    vmem = pl.BlockSpec(memory_space=pltpu.VMEM)
    bf16 = jnp.bfloat16
    return pl.pallas_call(
        kernel,
        out_shape=jax.ShapeDtypeStruct((BLOCK, DEPTH), bf16),
        in_specs=[any_space],
        out_specs=vmem,
        scratch_shapes=[
            pltpu.VMEM((4, BLOCK, DEPTH), bf16),
            pltpu.VMEM((2, 3, CHUNK, WIDE), bf16),
            pltpu.VMEM((2, CHUNK, FULL), bf16),
            pltpu.VMEM((2, CHUNK, WIDE), bf16),
            pltpu.VMEM((2, 2, CHUNK, WIDE), bf16),
            pltpu.VMEM((2, 3, CHUNK, PIECE), bf16),
            pltpu.VMEM((4, 4, CHUNK, FULL), bf16),
            pltpu.VMEM((4, BLOCK, DEPTH), bf16),
            pltpu.VMEM((BLOCK, DEPTH), jnp.float32),
            pltpu.VMEM((352, DEPTH), jnp.float32),
            pltpu.SemaphoreType.DMA,
            pltpu.SemaphoreType.DMA((COPIES,)),
            pltpu.SemaphoreType.DMA((COPIES,)),
        ],
        compiler_params=pltpu.CompilerParams(
            collective_id=0, has_side_effects=True, vmem_limit_bytes=63 * 2**20
        ),
        name="newton_schulz",
    )(iterate)


def solution(mesh):
    return jax.shard_map(
        on_device,
        mesh=mesh,
        in_specs=(P(("layer", "row"), "col"),),
        out_specs=P(("layer", "row"), "col"),
        check_vma=False,
    )
```

time: 242 us -> 221 us (0.913)
  Pallas kernels: 238 us -> 218 us
    pallas_call x1, Pallas kernels: 238 us -> 218 us  [on_device(): pl.pallas_call(kernel, out_shape=jax.ShapeDtypeStruct((BLOCK, DEPTH), bf1...]
where the time goes in v3:
time: 221 us
  Pallas kernels  218 us (99%)
  local copies, waits for them, and re-layouts  3.02 us (1%)
    pallas_call x1, Pallas kernels, on_device(): pl.pallas_call(kernel, out_shape=jax.ShapeDtypeStruct((BLOCK, DEPTH), bf1...  218 us

profile of v3, /device:TPU:0, one launch (start us, length us, event | category | flops | bytes accessed | tf_op | source)
XLA Modules:
  0.0 220.6 jit_solution(7560326314580637273)
XLA Ops:
  0.0 217.6 %newton_schulz.1 = bf16[1344,768]{1,0:T(8,128)(2,1)} custom-call(bf16[1344,768]{1,0:T(8,128)(2,1)} %x_hbm.1), custom_call_target="tpu_custom_call" | custom-call | tf_op jit(solution)/shard_map/newton_schulz/pallas_call | solution.py:440
  217.6 3.0 %copy.3 = bf16[1344,768]{1,0:T(8,128)(2,1)} copy(bf16[1344,768]{1,0:T(8,128)(2,1)} %newton_schulz.1) | data formatting | bytes 4128768

commit v4 on v3

--- a/solution.py
+++ b/solution.py
@@ -41,7 +41,7 @@
 
 
 def kernel(
-    x_hbm, o_ref, xs, send, summed, got_far, got_near, got_piece, gram, ys, acc, y_acc,
+    x_hbm, o_ref, xs, send, summed, got_far, got_near, got_piece, handed, gram, ys, acc, y_acc,
     local_sem, send_sem, recv_sem,
 ):
     layer = lax.axis_index("layer")
@@ -105,6 +105,7 @@
     down_low = start(x_hbm.at[low], xs.at[1, low], device(dz=-1))
     up_high = start(x_hbm.at[high], xs.at[3, high], device(dz=1))
     down_high = start(x_hbm.at[high], xs.at[1, high], device(dz=-1))
+    up_low = start(x_hbm.at[low], xs.at[3, low], device(dz=1))
 
     for k in range(2):
         summed[k, :, pl.ds(1280, FULL - 1280)] = jnp.zeros((CHUNK, FULL - 1280), jnp.bfloat16)
@@ -120,8 +121,9 @@
         )
 
     def gram_terms(slot, j, columns):
+        left, right = (3, 1) if j == 2 else (0, j)
         return lax.dot_general(
-            slot_rows(xs, 0, slot), xs[j, columns, :], TRANSPOSED,
+            slot_rows(xs, left, slot), xs[right, columns, :], TRANSPOSED,
             preferred_element_type=jnp.float32,
         )
 
@@ -235,20 +237,26 @@
             value = summed[k, rows, piece(place)].astype(jnp.float32)
             for step in range(3):
                 value = value + got_piece[k, step, rows, :].astype(jnp.float32)
-            gram[0, j, rows, piece(place)] = value.astype(jnp.bfloat16)
-        if j == 1:
+            value = value.astype(jnp.bfloat16)
+            if j == 2:
+                handed[rows, :] = value
+            else:
+                gram[0, j, rows, piece(place)] = value
+        if j != 0:
+            shared[j] = []
             for part, place in ((PART_A, pb), (PART_B, pa)):
                 rows = rows_of(part)
-                mirrored.append(
-                    start(
-                        gram.at[0, 1, rows, piece(place)],
-                        gram.at[0, 3, rows, piece(place)],
-                        device(dz=1),
-                    )
-                )
-        spread(j)
-
-    mirrored = []
+                if j == 1:
+                    src, theirs, way = gram.at[0, 1, rows, piece(place)], 3, 1
+                else:
+                    src, theirs, way = handed.at[rows], 2, -1
+                shared[j].append(
+                    start(src, gram.at[0, theirs, rows, piece(place)], device(dz=way))
+                )
+        if j != 2:
+            spread(j)
+
+    shared = {}
 
     def phase5(j, half):
         if half == 0:
@@ -376,7 +384,6 @@
     phase1(1, 0)
     received([up_high])
     far_high = start(xs.at[3, high], xs.at[2, high], device(dz=1))
-    up_low = start(x_hbm.at[low], xs.at[3, low], device(dz=1))
     phase4(0)
     phase2(1, 0)
     phase5(0, 0)
@@ -385,30 +392,31 @@
     phase1(1, 1)
     phase6(0, 0)
     phase6(0, 1)
-    received([far_high])
+    received([up_low])
+    phase1(2, 0)
     phase1(2, 1)
     phase2(1, 1)
     phase3(1)
+    phase2(2, 0)
     phase2(2, 1)
     phase4(1)
-    received([far_low])
-    phase1(2, 0)
-    received(mirrored)
+    phase3(2)
+    received(shared[1])
     spread(3)
-    phase2(2, 0)
+    phase4(2)
     phase5(3, 0)
     phase5(3, 1)
-    phase3(2)
+    received(shared[2])
+    spread(2)
     phase6(3, 0)
     phase6(3, 1)
-    phase4(2)
     phase5(1, 0)
+    phase5(2, 0)
     phase5(1, 1)
-    received([up_low])
+    phase5(2, 1)
     received(step6[3])
     once_mirrored()
-    phase5(2, 0)
-    phase5(2, 1)
+    received([far_low, far_high])
     received(step6[0])
     once("own", ((0, PART_A), (0, PART_B)))
     phase6(1, 0)
@@ -449,6 +457,7 @@
             pltpu.VMEM((2, CHUNK, WIDE), bf16),
             pltpu.VMEM((2, 2, CHUNK, WIDE), bf16),
             pltpu.VMEM((2, 3, CHUNK, PIECE), bf16),
+            pltpu.VMEM((CHUNK, PIECE), bf16),
             pltpu.VMEM((4, 4, CHUNK, FULL), bf16),
             pltpu.VMEM((4, BLOCK, DEPTH), bf16),
             pltpu.VMEM((BLOCK, DEPTH), jnp.float32),

time: 221 us -> 224 us (1.014)
    pallas_call x1, Pallas kernels: 218 us -> 220 us  [on_device(): pl.pallas_call(kernel, out_shape=jax.ShapeDtypeStruct((BLOCK, DEPTH), bf1...]
where the time goes in v4:
time: 224 us; the launch traced here: 223 us
  Pallas kernels  220 us (98%)
  local copies, waits for them, and re-layouts  3.02 us (1%)
    pallas_call x1, Pallas kernels, on_device(): pl.pallas_call(kernel, out_shape=jax.ShapeDtypeStruct((BLOCK, DEPTH), bf1...  220 us

profile of v4, /device:TPU:0, one launch (start us, length us, event | category | flops | bytes accessed | tf_op | source)
XLA Modules:
  0.0 223.4 jit_solution(9793411941622396331)
XLA Ops:
  0.0 220.4 %newton_schulz.1 = bf16[1344,768]{1,0:T(8,128)(2,1)} custom-call(bf16[1344,768]{1,0:T(8,128)(2,1)} %x_hbm.1), custom_call_target="tpu_custom_call" | custom-call | tf_op jit(solution)/shard_map/newton_schulz/pallas_call | solution.py:448
  220.4 3.0 %copy.3 = bf16[1344,768]{1,0:T(8,128)(2,1)} copy(bf16[1344,768]{1,0:T(8,128)(2,1)} %newton_schulz.1) | data formatting | bytes 4128768

commit v5 on v4

--- a/solution.py
+++ b/solution.py
@@ -85,9 +85,13 @@
             copy.wait_send()
             unsent[:] = [other for other in unsent if other is not copy]
 
+    landed = []
+
     def received(copies):
         for copy in copies:
-            copy.wait_recv()
+            if not any(other is copy for other in landed):
+                landed.append(copy)
+                copy.wait_recv()
 
     partners = [device(dz=1), device(dz=-1)]
     for step in (1, 2, 3):
@@ -296,30 +300,18 @@
             preferred_element_type=jnp.float32,
         )
 
-    def once_mirrored():
-        acc[...] = mirrored_terms(0, xs)
-
-        def add(slot, carry):
-            acc[...] += mirrored_terms(slot, xs)
-            return carry
-
-        lax.fori_loop(1, 4, add, 0)
+    def once_mirrored(slot, first=False):
+        terms = mirrored_terms(slot, xs)
+        acc[...] = terms if first else acc[...] + terms
+
+    def once_add(j, pieces):
+        left = [gram[slot, j, rows_of(part), body] for slot, part in pieces]
+        left = left[0] if len(left) == 1 else jnp.concatenate(left, axis=0)
+        term = jnp.dot(left, xs[j], preferred_element_type=jnp.float32)
+        rows = pl.ds(0, sum(part[1] for _, part in pieces))
+        y_acc[rows, :] = term if j == 0 else y_acc[rows, :] + term
 
     def once(name, pieces):
-        total = sum(part[1] for _, part in pieces)
-
-        def terms(j):
-            left = [gram[slot, j, rows_of(part), body] for slot, part in pieces]
-            left = left[0] if len(left) == 1 else jnp.concatenate(left, axis=0)
-            return jnp.dot(left, xs[j], preferred_element_type=jnp.float32)
-
-        y_acc[pl.ds(0, total), :] = terms(0)
-
-        def add(j, carry):
-            y_acc[pl.ds(0, total), :] += terms(j)
-            return carry
-
-        lax.fori_loop(1, 3, add, 0)
         offset = 0
         for slot, part in pieces:
             place = place_of(slot, part)
@@ -374,6 +366,11 @@
 
         lax.fori_loop(0, 4, add, 0)
 
+    slot_own = ((0, PART_A), (0, PART_B))
+    slot_first = ((1, HALF_AA), (3, HALF_AA), (1, HALF_BA), (3, HALF_BA))
+    slot_second = ((1, HALF_AB), (3, HALF_AB), (1, HALF_BB), (3, HALF_BB))
+    slot_last = ((2, PART_A), (2, PART_B))
+
     phase1(0, 0)
     phase1(0, 1)
     phase2(0, 0)
@@ -386,12 +383,8 @@
     far_high = start(xs.at[3, high], xs.at[2, high], device(dz=1))
     phase4(0)
     phase2(1, 0)
-    phase5(0, 0)
-    phase5(0, 1)
     received([down_high])
     phase1(1, 1)
-    phase6(0, 0)
-    phase6(0, 1)
     received([up_low])
     phase1(2, 0)
     phase1(2, 1)
@@ -400,36 +393,48 @@
     phase2(2, 0)
     phase2(2, 1)
     phase4(1)
+    received(step4[0])
     phase3(2)
     received(shared[1])
     spread(3)
     phase4(2)
     phase5(3, 0)
     phase5(3, 1)
+    once_add(0, slot_own)
+    once_mirrored(0, first=True)
     received(shared[2])
     spread(2)
     phase6(3, 0)
     phase6(3, 1)
+    received(step4[1])
+    once_add(1, slot_own)
+    phase5(0, 0)
     phase5(1, 0)
+    once_mirrored(1)
+    once_mirrored(3)
     phase5(2, 0)
+    received([far_low, far_high])
+    once_add(2, slot_own)
+    phase5(0, 1)
     phase5(1, 1)
     phase5(2, 1)
     received(step6[3])
-    once_mirrored()
-    received([far_low, far_high])
-    received(step6[0])
-    once("own", ((0, PART_A), (0, PART_B)))
-    phase6(1, 0)
-    phase6(2, 0)
-    once("first", ((1, HALF_AA), (3, HALF_AA), (1, HALF_BA), (3, HALF_BA)))
+    once_mirrored(2)
+    once("own", slot_own)
+    for j in range(3):
+        phase6(j, 0)
+        once_add(j, slot_first)
+    once("first", slot_first)
     pass_on("own")
-    phase6(1, 1)
-    phase6(2, 1)
-    once("second", ((1, HALF_AB), (3, HALF_AB), (1, HALF_BB), (3, HALF_BB)))
+    for j in range(3):
+        phase6(j, 1)
+        once_add(j, slot_second)
+    once("second", slot_second)
     pass_on("first")
-    received(step6[1])
-    received(step6[2])
-    once("last", ((2, PART_A), (2, PART_B)))
+    for j in range(3):
+        received(step6[j])
+        once_add(j, slot_last)
+    once("last", slot_last)
     pass_on("second")
     twice(0)
     pass_on("last")

time: 224 us -> 213 us (0.951)
  Pallas kernels: 220 us -> 208 us
    pallas_call x1, Pallas kernels: 220 us -> 208 us  [on_device(): pl.pallas_call(kernel, out_shape=jax.ShapeDtypeStruct((BLOCK, DEPTH), bf1...]
where the time goes in v5:
time: 213 us; the launch traced here: 211 us
  Pallas kernels  208 us (98%)
  local copies, waits for them, and re-layouts  3.02 us (1%)
    pallas_call x1, Pallas kernels, on_device(): pl.pallas_call(kernel, out_shape=jax.ShapeDtypeStruct((BLOCK, DEPTH), bf1...  208 us

profile of v5, /device:TPU:0, one launch (start us, length us, event | category | flops | bytes accessed | tf_op | source)
XLA Modules:
  0.0 211.1 jit_solution(17437975285731208368)
XLA Ops:
  0.0 208.1 %newton_schulz.1 = bf16[1344,768]{1,0:T(8,128)(2,1)} custom-call(bf16[1344,768]{1,0:T(8,128)(2,1)} %x_hbm.1), custom_call_target="tpu_custom_call" | custom-call | tf_op jit(solution)/shard_map/newton_schulz/pallas_call | solution.py:453
  208.1 3.0 %copy.3 = bf16[1344,768]{1,0:T(8,128)(2,1)} copy(bf16[1344,768]{1,0:T(8,128)(2,1)} %newton_schulz.1) | data formatting | bytes 4128768

commit v6 on v5

--- a/solution.py
+++ b/solution.py
@@ -18,7 +18,7 @@
 
 BLOCK = 1344
 CHUNK = 336
-SPLIT = 640
+THIRDS = ((0, 512, 512), (512, 512, 512), (1024, 320, 384))
 DEPTH = 768
 WIDE = 1408
 PIECE = 384
@@ -33,7 +33,7 @@
 
 TRANSPOSED = (((1,), (1,)), ((), ()))
 LEFT_TRANSPOSED = (((0,), (0,)), ((), ()))
-COPIES = 200
+COPIES = 230
 
 
 def rows_of(part):
@@ -105,29 +105,52 @@
     own.start()
     pl.semaphore_wait(barrier, len(partners))
 
-    low, high = pl.ds(0, SPLIT), pl.ds(SPLIT, BLOCK - SPLIT)
-    down_low = start(x_hbm.at[low], xs.at[1, low], device(dz=-1))
-    up_high = start(x_hbm.at[high], xs.at[3, high], device(dz=1))
-    down_high = start(x_hbm.at[high], xs.at[1, high], device(dz=-1))
-    up_low = start(x_hbm.at[low], xs.at[3, low], device(dz=1))
+    def place_of(slot, part):
+        position = pa if part[0] < PART_B[0] else pb
+        return pl.ds(pl.multiple_of(ring(position, slot) * CHUNK + part[0], 16), part[1])
+
+    columns = [pl.ds(first, count) for first, count, _ in THIRDS]
+    wide_columns = [pl.ds(first, count) for first, _, count in THIRDS]
+    from_next, from_last = {}, {}
+
+    def send_down(h):
+        from_next[h] = [start(x_hbm.at[columns[h]], xs.at[1, columns[h]], device(dz=-1))]
+
+    def send_up(slot):
+        from_last[slot] = []
+        for part in (PART_A, PART_B):
+            place = place_of(slot, part)
+            from_last[slot].append(start(x_hbm.at[place], xs.at[3, place], device(dz=1)))
+
+    send_down(0)
+    send_up(2)
+    send_down(1)
+    send_up(1)
+    send_up(3)
+    send_down(2)
+    send_up(0)
 
     for k in range(2):
         summed[k, :, pl.ds(1280, FULL - 1280)] = jnp.zeros((CHUNK, FULL - 1280), jnp.bfloat16)
     own.wait()
 
-    def place_of(slot, part):
-        position = pa if part[0] < PART_B[0] else pb
-        return pl.ds(pl.multiple_of(ring(position, slot) * CHUNK + part[0], 16), part[1])
+    far = []
+
+    def send_far(j, slot):
+        for part in (PART_A, PART_B):
+            place = place_of(slot, part)
+            way = device(dz=1) if j == 3 else device(dz=-1)
+            far.append(start(xs.at[j, place], xs.at[2, place], way))
 
     def slot_rows(ref, j, slot):
         return jnp.concatenate(
             [ref[j, place_of(slot, PART_A), :], ref[j, place_of(slot, PART_B), :]], axis=0
         )
 
-    def gram_terms(slot, j, columns):
+    def gram_terms(slot, j, h):
         left, right = (3, 1) if j == 2 else (0, j)
         return lax.dot_general(
-            slot_rows(xs, left, slot), xs[right, columns, :], TRANSPOSED,
+            slot_rows(xs, left, slot), xs[right, columns[h], :], TRANSPOSED,
             preferred_element_type=jnp.float32,
         )
 
@@ -136,8 +159,6 @@
     step1, step2, step3, step4, step5, step6 = {}, {}, {}, {}, {}, {}
     body = pl.ds(0, BLOCK)
     wide = pl.ds(0, WIDE)
-    halves = (low, high)
-    wide_halves = (low, pl.ds(SPLIT, WIDE - SPLIT))
 
     def reuse(name, j):
         key = name, buffer_set[j]
@@ -151,7 +172,7 @@
     def phase1(j, h):
         k = buffer_set[j]
         copies = reuse("far", j)
-        send[k, 0, :, halves[h]] = gram_terms(2, j, halves[h]).astype(jnp.bfloat16)
+        send[k, 0, :, columns[h]] = gram_terms(2, j, h).astype(jnp.bfloat16)
         step1[j, h] = []
         for half, target in (
             (HALF_AA, device(da=1)),
@@ -162,8 +183,8 @@
             rows = rows_of(half)
             step1[j, h].append(
                 start(
-                    send.at[k, 0, rows, wide_halves[h]],
-                    got_far.at[k, rows, wide_halves[h]],
+                    send.at[k, 0, rows, wide_columns[h]],
+                    got_far.at[k, rows, wide_columns[h]],
                     target,
                 )
             )
@@ -175,19 +196,19 @@
         step2[j, h] = []
         for side, slot, added in ((1, 1, (HALF_AA, HALF_BA)), (2, 3, (HALF_AB, HALF_BB))):
             copies = reuse(side, j)
-            terms = gram_terms(slot, j, halves[h])
+            terms = gram_terms(slot, j, h)
             for half in (HALF_AA, HALF_AB, HALF_BA, HALF_BB):
                 rows = rows_of(half)
                 value = terms[half[0] : half[0] + half[1], :]
                 if half in added:
-                    value = value + got_far[k, rows, halves[h]].astype(jnp.float32)
-                send[k, side, rows, halves[h]] = value.astype(jnp.bfloat16)
+                    value = value + got_far[k, rows, columns[h]].astype(jnp.float32)
+                send[k, side, rows, columns[h]] = value.astype(jnp.bfloat16)
             way = 1 if slot == 1 else -1
             for part, target in ((PART_A, device(da=way)), (PART_B, device(db=way))):
                 rows = rows_of(part)
                 copy = start(
-                    send.at[k, side, rows, wide_halves[h]],
-                    got_near.at[k, side - 1, rows, wide_halves[h]],
+                    send.at[k, side, rows, wide_columns[h]],
+                    got_near.at[k, side - 1, rows, wide_columns[h]],
                     target,
                 )
                 copies.append(copy)
@@ -199,13 +220,13 @@
     def phase3(j):
         k = buffer_set[j]
         copies = reuse("sum", j)
-        for h in (0, 1):
-            terms = gram_terms(0, j, halves[h])
+        for h in range(3):
+            terms = gram_terms(0, j, h)
             received(step2[j, h])
-            summed[k, :, halves[h]] = (
+            summed[k, :, columns[h]] = (
                 terms
-                + got_near[k, 0, :, halves[h]].astype(jnp.float32)
-                + got_near[k, 1, :, halves[h]].astype(jnp.float32)
+                + got_near[k, 0, :, columns[h]].astype(jnp.float32)
+                + got_near[k, 1, :, columns[h]].astype(jnp.float32)
             ).astype(jnp.bfloat16)
         step3[j] = []
         for step in (2, 1, 3):
@@ -319,29 +340,27 @@
             offset += part[1]
             acc[place, :] = coef_linear * xs[0, place, :].astype(jnp.float32) + coef_cubic * value
             ys[0, place, :] = value.astype(jnp.bfloat16)
-        direct[name] = []
-        for slot, part in pieces:
-            place = place_of(slot, part)
-            src = ys.at[0, place]
-            direct[name].append(
-                (
-                    slot,
-                    part,
-                    start(src, ys.at[3, place], device(dz=1)),
-                    start(src, ys.at[1, place], device(dz=-1)),
-                )
-            )
+        first = [p for p in pieces if p[1][0] < PART_B[0]]
+        second = [p for p in pieces if p[1][0] >= PART_B[0]]
+        direct[name] = {}
+        for ups, downs in ((first, second), (second, first)):
+            for way, block, group in ((1, 3, ups), (-1, 1, downs)):
+                for slot, part in group:
+                    place = place_of(slot, part)
+                    direct[name][way, slot, part] = start(
+                        ys.at[0, place], ys.at[block, place], device(dz=way)
+                    )
 
     def pass_on(name):
         forward[name] = []
-        for slot, part, up, down in direct[name]:
-            place = place_of(slot, part)
-            received([up, down])
-            if part[0] < PART_B[0]:
-                copy = start(ys.at[3, place], ys.at[2, place], device(dz=1))
-            else:
-                copy = start(ys.at[1, place], ys.at[2, place], device(dz=-1))
-            forward[name].append(copy)
+        for (way, slot, part), copy in direct[name].items():
+            if (part[0] < PART_B[0]) == (way == 1):
+                received([copy])
+                place = place_of(slot, part)
+                block = 3 if way == 1 else 1
+                forward[name].append(
+                    start(ys.at[block, place], ys.at[2, place], device(dz=way))
+                )
 
     def twice(j, last=False):
         def add(slot, carry):
@@ -359,39 +378,44 @@
 
         lax.fori_loop(0, 4, add, 0)
 
-    def twice_mirrored():
-        def add(slot, carry):
-            acc[...] += coef_quintic * mirrored_terms(slot, ys)
-            return carry
-
-        lax.fori_loop(0, 4, add, 0)
+    def twice_mirrored(slot):
+        acc[...] += coef_quintic * mirrored_terms(slot, ys)
 
     slot_own = ((0, PART_A), (0, PART_B))
     slot_first = ((1, HALF_AA), (3, HALF_AA), (1, HALF_BA), (3, HALF_BA))
     slot_second = ((1, HALF_AB), (3, HALF_AB), (1, HALF_BB), (3, HALF_BB))
     slot_last = ((2, PART_A), (2, PART_B))
 
-    phase1(0, 0)
-    phase1(0, 1)
-    phase2(0, 0)
-    phase2(0, 1)
+    for h in range(3):
+        phase1(0, h)
+    for h in range(3):
+        phase2(0, h)
     phase3(0)
-    received([down_low])
-    far_low = start(xs.at[1, low], xs.at[2, low], device(dz=-1))
+    received(from_next[0])
     phase1(1, 0)
-    received([up_high])
-    far_high = start(xs.at[3, high], xs.at[2, high], device(dz=1))
     phase4(0)
+    received(from_last[2])
+    phase1(2, 0)
     phase2(1, 0)
-    received([down_high])
+    received(from_next[1])
     phase1(1, 1)
-    received([up_low])
-    phase1(2, 0)
+    received(from_last[1])
+    received(from_last[3])
+    send_far(3, 2)
+    send_far(3, 1)
+    phase2(2, 0)
     phase1(2, 1)
     phase2(1, 1)
+    phase2(2, 1)
+    received(from_next[2])
+    phase1(1, 2)
+    send_far(1, 3)
+    send_far(1, 0)
+    phase1(2, 2)
+    phase2(1, 2)
     phase3(1)
-    phase2(2, 0)
-    phase2(2, 1)
+    received(from_last[0])
+    phase2(2, 2)
     phase4(1)
     received(step4[0])
     phase3(2)
@@ -413,7 +437,7 @@
     once_mirrored(1)
     once_mirrored(3)
     phase5(2, 0)
-    received([far_low, far_high])
+    received(far)
     once_add(2, slot_own)
     phase5(0, 1)
     phase5(1, 1)
@@ -437,8 +461,14 @@
     once("last", slot_last)
     pass_on("second")
     twice(0)
+    for name in ("own", "first", "second"):
+        received(direct[name].values())
+    twice_mirrored(0)
+    twice_mirrored(1)
+    twice_mirrored(3)
     pass_on("last")
-    twice_mirrored()
+    received(direct["last"].values())
+    twice_mirrored(2)
     twice(1)
     for name in ("own", "first", "second", "last"):
         received(forward[name])

time: 213 us -> 206 us (0.967)
  Pallas kernels: 208 us -> 200 us
    pallas_call x1, Pallas kernels: 208 us -> 200 us  [on_device(): pl.pallas_call(kernel, out_shape=jax.ShapeDtypeStruct((BLOCK, DEPTH), bf1...]
where the time goes in v6:
time: 206 us; the launch traced here: 203 us
  Pallas kernels  200 us (97%)
  local copies, waits for them, and re-layouts  3.02 us (1%)
    pallas_call x1, Pallas kernels, on_device(): pl.pallas_call(kernel, out_shape=jax.ShapeDtypeStruct((BLOCK, DEPTH), bf1...  200 us

profile of v6, /device:TPU:0, one launch (start us, length us, event | category | flops | bytes accessed | tf_op | source)
XLA Modules:
  0.0 203.4 jit_solution(7780348808741436207)
XLA Ops:
  0.0 200.4 %newton_schulz.1 = bf16[1344,768]{1,0:T(8,128)(2,1)} custom-call(bf16[1344,768]{1,0:T(8,128)(2,1)} %x_hbm.1), custom_call_target="tpu_custom_call" | custom-call | tf_op jit(solution)/shard_map/newton_schulz/pallas_call | solution.py:483
  200.4 3.0 %copy.3 = bf16[1344,768]{1,0:T(8,128)(2,1)} copy(bf16[1344,768]{1,0:T(8,128)(2,1)} %newton_schulz.1) | data formatting | bytes 4128768

commit v7 on v6

--- a/solution.py
+++ b/solution.py
@@ -33,7 +33,7 @@
 
 TRANSPOSED = (((1,), (1,)), ((), ()))
 LEFT_TRANSPOSED = (((0,), (0,)), ((), ()))
-COPIES = 230
+COPIES = 250
 
 
 def rows_of(part):
@@ -41,7 +41,8 @@
 
 
 def kernel(
-    x_hbm, o_ref, xs, send, summed, got_far, got_near, got_piece, handed, gram, ys, acc, y_acc,
+    x_hbm, o_ref, xs, send, summed, got_far, got_near, relayed, got_piece, handed, gram, ys, acc,
+    y_acc,
     local_sem, send_sem, recv_sem,
 ):
     layer = lax.axis_index("layer")
@@ -156,7 +157,12 @@
 
     buffer_set = {0: 0, 1: 1, 2: 0}
     from_buffer = {}
-    step1, step2, step3, step4, step5, step6 = {}, {}, {}, {}, {}, {}
+    step1, step2, step3, step3_on = {}, {}, {}, {}
+    step4, step4_on, step5, step6 = {}, {}, {}, {}
+    second_rings = (
+        ((HALF_AA, HALF_AB), pb, lambda way: device(db=way)),
+        ((HALF_BA, HALF_BB), pa, lambda way: device(da=way)),
+    )
     body = pl.ds(0, BLOCK)
     wide = pl.ds(0, WIDE)
 
@@ -229,39 +235,59 @@
                 + got_near[k, 1, :, columns[h]].astype(jnp.float32)
             ).astype(jnp.bfloat16)
         step3[j] = []
-        for step in (2, 1, 3):
-            for part, place, target in (
-                (PART_A, ring(pb, step), device(db=step)),
-                (PART_B, ring(pa, step), device(da=step)),
-            ):
+        for halves, position, ring_device in second_rings:
+            place = piece(ring(position, 2))
+            for half, way in zip(halves, (1, -1)):
+                rows = rows_of(half)
+                step3[j].append(
+                    start(summed.at[k, rows, place], relayed.at[k, rows], ring_device(way))
+                )
+        copies += step3[j]
+
+    def phase3_on(j):
+        k = buffer_set[j]
+        received(step3[j])
+        step3_on[j] = []
+        for (_, position, ring_device), part in zip(second_rings, (PART_A, PART_B)):
+            for side, way in enumerate((1, -1)):
+                place = piece(ring(position, way))
+                half = second_rings[part == PART_B][0][side]
+                rows = rows_of(half)
+                summed[k, rows, place] = (
+                    summed[k, rows, place].astype(jnp.float32)
+                    + relayed[k, rows, :].astype(jnp.float32)
+                ).astype(jnp.bfloat16)
                 rows = rows_of(part)
-                step3[j].append(
+                step3_on[j].append(
                     start(
-                        summed.at[k, rows, piece(place)],
-                        got_piece.at[k, step - 1, rows],
-                        target,
+                        summed.at[k, rows, place], got_piece.at[k, side, rows], ring_device(way)
                     )
                 )
-        copies += step3[j]
+        from_buffer["sum", k][1].extend(step3_on[j])
 
     def spread(j):
         step4[j] = []
-        for step in (2, 1, 3):
-            for part, place, target in (
-                (PART_A, pb, device(db=step)),
-                (PART_B, pa, device(da=step)),
-            ):
-                where = gram.at[0, j, rows_of(part), piece(place)]
-                step4[j].append(start(where, where, target))
+        for (_, position, ring_device), part in zip(second_rings, (PART_A, PART_B)):
+            where = gram.at[0, j, rows_of(part), piece(position)]
+            for way in (1, -1):
+                step4[j].append(start(where, where, ring_device(way)))
+
+    def spread_on(j):
+        received(step4[j])
+        step4_on[j] = []
+        for halves, position, ring_device in second_rings:
+            for half, way in zip(halves, (1, -1)):
+                where = gram.at[0, j, rows_of(half), piece(ring(position, -way))]
+                step4_on[j].append(start(where, where, ring_device(way)))
 
     def phase4(j):
         k = buffer_set[j]
-        received(step3[j])
+        received(step3_on[j])
         for part, place in ((PART_A, pb), (PART_B, pa)):
             rows = rows_of(part)
             value = summed[k, rows, piece(place)].astype(jnp.float32)
-            for step in range(3):
-                value = value + got_piece[k, step, rows, :].astype(jnp.float32)
+            for side in range(2):
+                value = value + got_piece[k, side, rows, :].astype(jnp.float32)
             value = value.astype(jnp.bfloat16)
             if j == 2:
                 handed[rows, :] = value
@@ -278,14 +304,14 @@
                 shared[j].append(
                     start(src, gram.at[0, theirs, rows, piece(place)], device(dz=way))
                 )
-        if j != 2:
+        if j == 0:
             spread(j)
 
     shared = {}
 
     def phase5(j, half):
         if half == 0:
-            received(step4[j])
+            received(step4_on[j])
             step5[j] = []
         copies = []
         for rows_half, target_up, target_down in (
@@ -393,44 +419,52 @@
     phase3(0)
     received(from_next[0])
     phase1(1, 0)
-    phase4(0)
+    phase3_on(0)
     received(from_last[2])
     phase1(2, 0)
     phase2(1, 0)
+    phase4(0)
     received(from_next[1])
     phase1(1, 1)
     received(from_last[1])
     received(from_last[3])
-    send_far(3, 2)
-    send_far(3, 1)
     phase2(2, 0)
     phase1(2, 1)
+    spread_on(0)
     phase2(1, 1)
     phase2(2, 1)
     received(from_next[2])
     phase1(1, 2)
-    send_far(1, 3)
-    send_far(1, 0)
     phase1(2, 2)
     phase2(1, 2)
     phase3(1)
     received(from_last[0])
     phase2(2, 2)
+    phase3_on(1)
+    phase3(2)
     phase4(1)
-    received(step4[0])
-    phase3(2)
+    phase3_on(2)
     received(shared[1])
     spread(3)
     phase4(2)
+    for slot in (2, 1):
+        send_far(3, slot)
+    for slot in (3, 0):
+        send_far(1, slot)
+    spread_on(3)
+    spread(1)
     phase5(3, 0)
     phase5(3, 1)
+    received(shared[2])
+    spread(2)
+    spread_on(1)
+    received(step4_on[0])
     once_add(0, slot_own)
     once_mirrored(0, first=True)
-    received(shared[2])
-    spread(2)
     phase6(3, 0)
+    spread_on(2)
     phase6(3, 1)
-    received(step4[1])
+    received(step4_on[1])
     once_add(1, slot_own)
     phase5(0, 0)
     phase5(1, 0)
@@ -447,14 +481,16 @@
     once("own", slot_own)
     for j in range(3):
         phase6(j, 0)
+        if j == 2:
+            pass_on("own")
         once_add(j, slot_first)
     once("first", slot_first)
-    pass_on("own")
     for j in range(3):
         phase6(j, 1)
+        if j == 2:
+            pass_on("first")
         once_add(j, slot_second)
     once("second", slot_second)
-    pass_on("first")
     for j in range(3):
         received(step6[j])
         once_add(j, slot_last)
@@ -491,7 +527,8 @@
             pltpu.VMEM((2, CHUNK, FULL), bf16),
             pltpu.VMEM((2, CHUNK, WIDE), bf16),
             pltpu.VMEM((2, 2, CHUNK, WIDE), bf16),
-            pltpu.VMEM((2, 3, CHUNK, PIECE), bf16),
+            pltpu.VMEM((2, CHUNK, PIECE), bf16),
+            pltpu.VMEM((2, 2, CHUNK, PIECE), bf16),
             pltpu.VMEM((CHUNK, PIECE), bf16),
             pltpu.VMEM((4, 4, CHUNK, FULL), bf16),
             pltpu.VMEM((4, BLOCK, DEPTH), bf16),

time: 206 us -> 200 us (0.971)
  Pallas kernels: 200 us -> 196 us
    pallas_call x1, Pallas kernels: 200 us -> 196 us  [on_device(): pl.pallas_call(kernel, out_shape=jax.ShapeDtypeStruct((BLOCK, DEPTH), bf1...]
where the time goes in v7:
time: 200 us; the launch traced here: 199 us
  Pallas kernels  196 us (98%)
  local copies, waits for them, and re-layouts  3.02 us (2%)
    pallas_call x1, Pallas kernels, on_device(): pl.pallas_call(kernel, out_shape=jax.ShapeDtypeStruct((BLOCK, DEPTH), bf1...  196 us

profile of v7, /device:TPU:0, one launch (start us, length us, event | category | flops | bytes accessed | tf_op | source)
XLA Modules:
  0.0 199.4 jit_solution(204758269788083806)
XLA Ops:
  0.0 196.4 %newton_schulz.1 = bf16[1344,768]{1,0:T(8,128)(2,1)} custom-call(bf16[1344,768]{1,0:T(8,128)(2,1)} %x_hbm.1), custom_call_target="tpu_custom_call" | custom-call | tf_op jit(solution)/shard_map/newton_schulz/pallas_call | solution.py:519
  196.4 3.0 %copy.3 = bf16[1344,768]{1,0:T(8,128)(2,1)} copy(bf16[1344,768]{1,0:T(8,128)(2,1)} %newton_schulz.1) | data formatting | bytes 4128768
